TPU v7x, 256 devices: a whole 4x4x8 slice. The times are simulated.
256 devices in a mesh: det: 16 (over x, z_lo, core), tm: 16 (over z_hi, y).
Axes of the slice: x: 4, y: 4, z: 8 (z_hi: 4, z_lo: 2; z = z_hi * 2 + z_lo), core: 2. Of those that a mesh axis runs over, the one named last changes fastest.
Arguments:
- sky_map: float32 [16384, 128], P('det'), may hold values from -6 to 6
- tile_slot: int32 [256, 24576], P('det', 'tm'), may hold values from 0 to 511
- pixel_offset: int32 [256, 24576], P('det', 'tm'), may hold values from 0 to 127
- tile_list: int32 [16, 16, 16, 32], P('det', 'tm'), may hold values from 0 to 1023, as said below
- noise_kernel: float32 [256, 65], P('det'), may hold values from -0.6 to 0.6
Outputs:
- normal_image: float32 [16384, 128], P('det')
Inputs may be any that keep to these rules, and one draw needn't show every extreme that they name: `tile_list`: for each detector group, time span and owner, the 32 entries are distinct tiles of that owner.
All inputs are finite; a program needn't handle non-finite values.
Results may differ from a plain program's by a relative error of at most 0.00007.
Values sent between devices are 32-bit elements; how exact they have to be, the bound alone decides.
A program may use at most 64 MiB of HBM per device.

v0:
```python
import jax
import jax.numpy as jnp
from jax import lax
from jax.sharding import PartitionSpec as P

PIX = 128
W = 64


def with_halo(cells, sides, width):
    for axis, dim in sides:
        count = lax.axis_size(axis)
        ends = count - 1
        head = lax.slice_in_dim(cells, 0, width, axis=dim)
        tail = lax.slice_in_dim(cells, cells.shape[dim] - width, cells.shape[dim], axis=dim)
        cells = jnp.concatenate(
            [
                lax.ppermute(tail, axis, [(i, (i + 1) % count) for i in range(ends)]),
                cells,
                lax.ppermute(head, axis, [((i + 1) % count, i) for i in range(ends)]),
            ],
            axis=dim,
        )
    return cells


def filter_rows(padded, noise_kernel):
    row_count, width = padded.shape
    length = width - 2 * W
    blocks = length // PIX
    pieces = (PIX + 2 * W) // PIX
    windows = jnp.stack(
        [
            padded[:, number * PIX : number * PIX + length].reshape(row_count, blocks, PIX)
            for number in range(pieces)
        ],
        axis=2,
    )
    windows = windows.reshape(row_count, blocks, pieces * PIX)
    lag_table = (
        jnp.arange(PIX + 2 * W, dtype=jnp.int32)[:, None]
        - W
        - jnp.arange(PIX, dtype=jnp.int32)[None, :]
    )
    distance = jnp.abs(lag_table)
    toeplitz = jnp.where(
        distance <= W,
        jnp.take(noise_kernel, jnp.minimum(distance, W), axis=1),
        jnp.zeros((), jnp.float32),
    )
    result = jnp.einsum("rbm,rmj->rbj", windows, toeplitz, precision=lax.Precision.HIGHEST)
    return result.reshape(row_count, length)


def blocked_filter(padded, noise_kernel):
    row_count, width = padded.shape
    group = 8
    grouped = padded.reshape(row_count // group, group, width)
    kernels = noise_kernel.reshape(row_count // group, group, W + 1)
    result = lax.map(lambda pair: filter_rows(pair[0], pair[1]), (grouped, kernels))
    return result.reshape(row_count, width - 2 * W)


def one_hot(values, count):
    return (values[:, None] == jnp.arange(count, dtype=jnp.int32)[None, :]).astype(jnp.float32)


def sample_blocks(tile_slot, pixel_offset):
    total = tile_slot.shape[0] * tile_slot.shape[1]
    block = 2048
    slots = tile_slot.reshape(total // block, block)
    offsets = pixel_offset.reshape(total // block, block)
    return (slots, offsets)


def read_samples(slot_rows, tile_slot, pixel_offset):
    slot_total = slot_rows.shape[0]
    slots, offsets = sample_blocks(tile_slot, pixel_offset)

    def read_one_block(pair):
        selector = one_hot(pair[0], slot_total)
        rows = jnp.dot(selector, slot_rows, precision=lax.Precision.HIGHEST)
        return jnp.sum(rows * one_hot(pair[1], PIX), axis=1)

    return lax.map(read_one_block, (slots, offsets)).reshape(tile_slot.shape)


def add_samples(filtered, tile_slot, pixel_offset, slot_total):
    slots, offsets = sample_blocks(tile_slot, pixel_offset)
    values = filtered.reshape(slots.shape)

    def add_one_block(carry, triple):
        spread = triple[2][:, None] * one_hot(triple[1], PIX)
        selector = one_hot(triple[0], slot_total)
        added = lax.dot_general(
            selector, spread, (((0,), (0,)), ((), ())), precision=lax.Precision.HIGHEST
        )
        return (carry + added, None)

    start = jnp.zeros((slot_total, PIX), jnp.float32)
    summed, unused = lax.scan(add_one_block, start, (slots, offsets, values))
    return summed


def on_device(sky_map, tile_slot, pixel_offset, tile_list, noise_kernel):
    owners = lax.axis_size("det")
    tiles_owned = sky_map.shape[0]
    slot_count = tile_list.shape[3]
    slot_total = owners * slot_count
    wanted = tile_list.reshape(owners, slot_count)
    whole = lax.all_gather(sky_map, "det", axis=0, tiled=True)
    global_rows = (wanted + jnp.arange(owners, dtype=jnp.int32)[:, None] * tiles_owned).reshape(-1)
    slot_rows = jnp.take(whole, global_rows, axis=0)
    samples = read_samples(slot_rows, tile_slot, pixel_offset)
    padded = with_halo(samples, (("tm", 1),), W)
    filtered = blocked_filter(padded, noise_kernel)
    slot_sums = add_samples(filtered, tile_slot, pixel_offset, slot_total)
    wide_sums = jnp.zeros((owners * tiles_owned, PIX), jnp.float32).at[global_rows].set(slot_sums)
    partial_value = lax.psum_scatter(wide_sums, "det", scatter_dimension=0, tiled=True)
    return lax.psum(partial_value, "tm")


def solution(mesh):
    return jax.shard_map(
        on_device,
        mesh=mesh,
        in_specs=(
            P("det", None),
            P("det", "tm"),
            P("det", "tm"),
            P("det", "tm", None, None),
            P("det", None),
        ),
        out_specs=P("det", None),
        check_vma=False,
    )
```

profile of v0, /device:TPU:32, one launch (start us, length us, event | category | flops | bytes accessed | tf_op | source)
XLA Modules:
  0.0 691.9 jit_solution(17800579621356285415)
XLA Ops:
  11.0 55.5 %all-gather.2.cloned.1.call-done = f32[16384,128]{1,0:T(8,128)} async-done(((f32[1024,128]{1,0:T(8,128)}), f32[16384,128]{1,0:T(8,128)}) %all-gather.2.cloned.1.call-update) | async-done | bytes 8388624 | tf_op jit(solution)/shard_map/all_gather | solution.py:111
  66.5 4.4 gather_fusion.1
  71.0 35.7 %while.33 = (s32[]{:T(128)}, f32[12,2048]{1,0:T(8,128)S(1)}, s32[12,2048]{1,0:T(8,128)S(1)}, s32[12,2048]{1,0:T(8,128)S(1)}, f32[512,128]{1,0:T(8,128)S(1)}, /*index=5*/s32[]{:T(128)}, s32[]{:T(128)}) while((s32[]{:T(128)}, f32[12,2048]{1,0:T(8,128)S(1)}, s32[12,2048]{1,0:T(8,128)S(1)}, s32[12,2048]{1,0:T(8,128)S(1)}, ...), condition=%wide.region_2.3_spmd, body=%wide.region_0.0_spmd.sunk | while | flops 1612445696 | bytes 335957 | solution.py:85
  71.1 2.7 fusion.43
  74.1 2.7 fusion.43
  77.0 2.7 fusion.43
  80.0 2.7 fusion.43
  83.0 2.7 fusion.43
  86.0 2.7 fusion.43
  106.8 3.4 collective-permute-start
  111.6 4.2 collective-permute-done.1
  115.9 238.6 %while.34 = (s32[]{:T(128)}, f32[2,8,1536]{2,1,0:T(8,128)S(1)}, f32[2,8,1664]{2,1,0:T(8,128)S(1)}, f32[2,8,65]{2,1,0:T(8,128)S(1)}, s32[]{:T(128)}) while((s32[]{:T(128)}, f32[2,8,1536]{2,1,0:T(8,128)S(1)}, f32[2,8,1664]{2,1,0:T(8,128)S(1)}, f32[2,8,65]{2,1,0:T(8,128)S(1)}, s32[]{:T(128)}) %tuple.87), condition=%wide.region_4.5_spmd, body=%wide.region_3.4_spmd.sunk | while | flops 38854912 | bytes 6491337 | solution.py:60
  116.2 108.5 %gather_fusion = f32[32768,8]{1,0:T(8,128)} fusion(f32[8,65]{0,1:T(8,128)S(1)} %bitcast.60, s32[32768]{0:T(1024)S(1)} %fusion.46), kind=kCustom, calls=%fused_computation.clone.1 | custom fusion | bytes 2228224 | tf_op jit(solution)/shard_map/while/body/eval_jaxpr/jit(_take)/gather | solution.py:48
  224.7 9.5 %copy.18 = f32[256,128,8]{1,0,2:T(8,128)S(1)} copy(f32[256,128,8]{2,1,0:T(8,128)} %bitcast.61) | data formatting | bytes 2097152 | tf_op jit(solution)/shard_map/while/body/eval_jaxpr/jit(_take)/gather | solution.py:48
  235.5 108.5 %gather_fusion = f32[32768,8]{1,0:T(8,128)} fusion(f32[8,65]{0,1:T(8,128)S(1)} %bitcast.60, s32[32768]{0:T(1024)S(1)} %fusion.46), kind=kCustom, calls=%fused_computation.clone.1 | custom fusion | bytes 2228224 | tf_op jit(solution)/shard_map/while/body/eval_jaxpr/jit(_take)/gather | solution.py:48
  344.0 9.5 %copy.18 = f32[256,128,8]{1,0,2:T(8,128)S(1)} copy(f32[256,128,8]{2,1,0:T(8,128)} %bitcast.61) | data formatting | bytes 2097152 | tf_op jit(solution)/shard_map/while/body/eval_jaxpr/jit(_take)/gather | solution.py:48
  354.5 52.7 %while.35 = (s32[]{:T(128)}, f32[512,128]{1,0:T(8,128)S(1)}, s32[12,2048]{1,0:T(8,128)S(1)}, s32[12,2048]{1,0:T(8,128)S(1)}, f32[12,2048]{1,0:T(8,128)S(1)}, /*index=5*/s32[]{:T(128)}, s32[]{:T(128)}) while((s32[]{:T(128)}, f32[512,128]{1,0:T(8,128)S(1)}, s32[12,2048]{1,0:T(8,128)S(1)}, s32[12,2048]{1,0:T(8,128)S(1)}, ...), condition=%wide.region_6.7_spmd.clone, body=%wide.region_5.6_spmd.clone.sunk | while | flops 1612316672 | bytes 598111 | solution.py:101
  354.6 4.3 fusion.50
  359.0 4.3 fusion.50
  363.4 4.3 fusion.50
  367.8 4.3 fusion.50
  372.2 4.3 fusion.50
  376.5 4.3 fusion.50
  380.9 4.3 fusion.50
  385.3 4.3 fusion.50
  389.7 4.3 fusion.50
  394.1 4.3 fusion.50
  398.5 4.3 fusion.50
  402.9 4.3 fusion.50
  407.2 5.4 scatter_custom_fusion
  412.7 100.7 %reduce-scatter.2.cloned.1.call-done = f32[1024,128]{1,0:T(8,128)} async-done(((f32[16384,128]{1,0:T(8,128)}), f32[1024,128]{1,0:T(8,128)}) %reduce-scatter.2.cloned.1.call-update) | async-done | bytes 524304 | tf_op jit(solution)/shard_map/reduce_scatter | solution.py:119
  513.4 170.1 %all-reduce.2.cloned.1.call-done = f32[1024,128]{1,0:T(8,128)} async-done(((f32[1024,128]{1,0:T(8,128)}), f32[1024,128]{1,0:T(8,128)}) %all-reduce.2.cloned.1.call-update) | async-done | bytes 524304 | tf_op jit(solution)/shard_map/psum | solution.py:120
  (107 shorter events, 29.8 us)
Async XLA Ops:
  6.5 60.0 %all-gather.2.cloned.1.call-start = ((), (), s32[]{:S(2)}) async-start(), calls=%async_computation.1 | async-start | bytes 8912896 | tf_op jit(solution)/shard_map/all_gather | solution.py:111
  7.3 506.1 %reduce-scatter.2.cloned.1.call-start = ((), (), s32[]{:S(2)}) async-start(), calls=%async_computation.2 | async-start | bytes 8912896 | tf_op jit(solution)/shard_map/reduce_scatter | solution.py:119
  11.0 104.9 %copy-start = (f32[16,65]{1,0:T(8,128)S(1)}, f32[16,65]{1,0:T(8,128)}, u32[]{:S(2)}) copy-start(f32[16,65]{1,0:T(8,128)} %param.15) | copy-start | bytes 12484
  106.8 4.7 collective-permute-start
  110.2 5.5 collective-permute-start.1
  412.7 270.8 %all-reduce.2.cloned.1.call-start = ((), (), s32[]{:S(2)}) async-start(), calls=%async_computation.3 | async-start | bytes 1048576 | tf_op jit(solution)/shard_map/psum | solution.py:120
Sparse Core Ops, SparseCore 0:
  9.2 57.2 all-gather.1
  412.8 100.5 reduce-scatter.1
  516.0 167.4 all-reduce.1
where the time goes:
time: 694 us; the launch traced here: 692 us
  waiting for transfers between devices  331 us (48%)
  local copies, waits for them, and re-layouts  255 us (37%)
  matrix products  85.8 us (12%)
  between operations  13.3 us (2%)
    gather x4, local copies, waits for them, and re-layouts, filter_rows(): jnp.take(noise_kernel, jnp.minimum(distance, W), axis=1)  236 us
    psum x1, waiting for transfers between devices, on_device(): return lax.psum(partial_value, 'tm')  170 us
    reduce_scatter x1, waiting for transfers between devices, on_device(): lax.psum_scatter(wide_sums, 'det', scatter_dimension=0, tiled=True)  101 us
    all_gather x1, waiting for transfers between devices, on_device(): whole = lax.all_gather(sky_map, 'det', axis=0, tiled=True)  55.5 us
    dot_general x12, matrix products, add_one_block(): lax.dot_general(selector, spread, (((0,), (0,)), ((), ())), precision=lax...  51.7 us
    dot_general x12, matrix products, read_one_block(): rows = jnp.dot(selector, slot_rows, precision=lax.Precision.HIGHEST)  32.5 us
  transfers between devices with their start and end apart: 5, of which 4 were waited for; matrix products, arithmetic and copies ran while one was open for 1% of the time, Pallas kernels for 0%

commit v1 on v0

v1 whole, which is shorter than its diff:
```python
import jax
import jax.numpy as jnp
from jax import lax
from jax.experimental import pallas as pl
from jax.experimental.pallas import tpu as pltpu
from jax.sharding import PartitionSpec as P

PIX = 128
W = 64
N_DET = 16
N_TM = 16
N_Y = 4
N_Z = 4
ROWS = 16
LENGTH = 1536
BLOCKS = LENGTH // PIX
TILES = 1024
SLOTS = 32
SLOT_ALL = N_DET * SLOTS
SUB = TILES // (N_Y * N_Z)
WIDE = ROWS * PIX

F32 = jnp.float32
BF16 = jnp.bfloat16
I32 = jnp.int32
NT = (((1,), (1,)), ((), ()))
MESH = pl.DeviceIdType.MESH


def halves(values):
    high = values.astype(BF16)
    low = (values - high.astype(F32)).astype(BF16)
    return high, low


def iota(shape, dim):
    return lax.broadcasted_iota(I32, shape, dim)


def one_hot(mask):
    return jnp.where(mask, 1.0, 0.0).astype(BF16)


def build_toeplitz(noise, toeplitz):
    width = 2 * PIX
    place = iota((PIX, width), 1)
    lag = iota((PIX, width), 0)
    pick = one_hot((jnp.abs(place - W) == lag) & (lag <= W))
    coeffs = jnp.concatenate([noise[...], jnp.zeros((ROWS, PIX - W - 1), F32)], axis=1)
    first, rest = halves(coeffs)
    spread = jnp.dot(first, pick, preferred_element_type=F32) + jnp.dot(rest, pick, preferred_element_type=F32)
    for row in range(ROWS):
        wide = jnp.broadcast_to(spread[row : row + 1, :], (PIX, width))
        rolled = pltpu.roll(wide, 0, 1, stride=1, stride_axis=0)
        high, low = halves(rolled)
        toeplitz[row, 0:PIX, :] = high
        toeplitz[row, PIX : 2 * PIX, :] = low


def build_one_hot(slot, selector):
    rank = iota((SLOT_ALL, PIX), 0)

    def step(block, carry):
        span = pl.ds(pl.multiple_of(block * PIX, PIX), PIX)
        for row in range(ROWS):
            selector[block, :, row * PIX : (row + 1) * PIX] = one_hot(rank == slot[row : row + 1, span])
        return carry

    lax.fori_loop(0, BLOCKS, step, 0)


def read_block(block, table, selector, off, store):
    rank = iota((PIX, PIX), 0)
    span = pl.ds(pl.multiple_of(block * PIX, PIX), PIX)
    for row in range(0, ROWS, 2):
        both = jnp.dot(table[...], selector[block, :, row * PIX : (row + 2) * PIX], preferred_element_type=F32)
        both = both[:PIX] + both[PIX:]
        for more in range(2):
            mask = rank == off[row + more : row + more + 1, span]
            part = both[:, more * PIX : (more + 1) * PIX]
            store(row + more, jnp.sum(jnp.where(mask, part, 0.0), axis=0, keepdims=True))


def filter_samples(samples, toeplitz, filtered):
    lane = iota((16, PIX), 1)
    for row in range(ROWS):
        turned = pltpu.roll(samples[row], W, 1)
        window = jnp.where(lane < W, turned, pltpu.roll(turned, 15, 0))
        window = jnp.concatenate([window, pltpu.roll(window, 15, 0)], axis=1)
        high, low = halves(window)
        out = lax.dot_general(jnp.concatenate([high, low], axis=0), toeplitz[row], NT, preferred_element_type=F32)
        filtered[row] = out[:16, :PIX] + out[:16, PIX:] + out[16:, :PIX]


def scatter_samples(filtered, off, selector, spread, total):
    rank = iota((PIX, PIX), 0)
    total[...] = jnp.zeros_like(total)

    def step(block, carry):
        span = pl.ds(pl.multiple_of(block * PIX, PIX), PIX)
        for row in range(ROWS):
            mask = rank == off[row : row + 1, span]
            value = filtered[row, pl.ds(block, 1), :]
            high = value.astype(BF16).astype(F32)
            cols = slice(row * PIX, (row + 1) * PIX)
            spread[0:PIX, cols] = jnp.where(mask, high, 0.0).astype(BF16)
            spread[PIX : 2 * PIX, cols] = jnp.where(mask, value - high, 0.0).astype(BF16)
        total[...] += lax.dot_general(selector[block], spread[...], NT, preferred_element_type=F32)
        return carry

    lax.fori_loop(0, BLOCKS, step, 0)


def kernel(
    sky_h, slot_h, off_h, list_h, noise_h, out_h,
    sky, slot, off, wanted, noise,
    req_out, req_in, rows_out, rows_in, edge_out, edge_in, sums_out, sums_in,
    sky_parts, pick_rows, pick_cols, image, part_y, sum_y, part_z, whole,
    toeplitz, selector, table, samples, filtered, spread, total,
    load_sem, req_s, req_r, rows_s, rows_r, edge_s, edge_r, sums_s, sums_r,
    ry_s, ry_r, rz_s, rz_r, gy_s, gy_r, gz_s, gz_r, save_sem,
):
    group = lax.axis_index("det")
    span = lax.axis_index("tm")
    y = lax.rem(span, N_Y)
    z = lax.div(span, N_Y)

    barrier = pltpu.get_barrier_semaphore()
    for step in range(1, N_DET):
        pl.semaphore_signal(barrier, inc=1, device_id=(lax.rem(group + step, N_DET), span), device_id_type=MESH)
    for step in range(1, N_TM):
        pl.semaphore_signal(barrier, inc=1, device_id=(group, lax.rem(span + step, N_TM)), device_id_type=MESH)

    loads = [
        pltpu.make_async_copy(source, target, load_sem.at[number])
        for number, (source, target) in enumerate(
            [(list_h, wanted), (sky_h, sky), (slot_h, slot), (noise_h, noise), (off_h, off)]
        )
    ]
    for load in loads:
        load.start()

    def remote(source, target, send, recv, device):
        copy = pltpu.make_async_remote_copy(
            src_ref=source, dst_ref=target, send_sem=send, recv_sem=recv, device_id=device, device_id_type=MESH
        )
        copy.start()
        return copy

    sent = []

    loads[0].wait()
    mine = wanted[0, 0]
    mine = jnp.concatenate([mine] * (PIX // SLOTS), axis=1)
    for owner in range(N_DET):
        req_out[owner] = jnp.broadcast_to(mine[owner : owner + 1, :], (8, PIX))
    pl.semaphore_wait(barrier, N_DET + N_TM - 2)
    requests = []
    for step in range(1, N_DET):
        owner = lax.rem(group + step, N_DET)
        requests.append(remote(req_out.at[owner], req_in.at[group], req_s.at[step], req_r.at[step], (owner, span)))
    req_in[group] = req_out[group]

    loads[1].wait()
    high, low = halves(sky[...])
    sky_parts[:, 0:PIX] = high
    sky_parts[:, PIX : 2 * PIX] = low
    for request in requests:
        request.wait_recv()

    lane = iota((1, PIX), 1)
    lists = []
    for four in range(4):
        row = req_in[4 * four, 0:1, :]
        for place in range(1, 4):
            row = jnp.where(lane >= place * SLOTS, req_in[4 * four + place, 0:1, :], row)
        lists.append(row)
    upright = jnp.concatenate(lists + [jnp.zeros((4, PIX), I32)], axis=0).T
    for four in range(4):
        chosen = upright[:, four : four + 1] == iota((PIX, TILES), 1)
        pick_rows[four * PIX : (four + 1) * PIX, :] = one_hot(chosen)
    both = jnp.dot(pick_rows[...], sky_parts[...], preferred_element_type=F32)
    rows_out[...] = (both[:, :PIX] + both[:, PIX:]).reshape(N_DET, SLOTS, PIX)
    tiles = []
    for step in range(1, N_DET):
        reader = lax.rem(group + step, N_DET)
        tiles.append(remote(rows_out.at[reader], rows_in.at[group], rows_s.at[step], rows_r.at[step], (reader, span)))
    rows_in[group] = rows_out[group]

    for four in range(4):
        pick_cols[:, four * PIX : (four + 1) * PIX] = one_hot(iota((TILES, PIX), 0) == lists[four])
    loads[2].wait()
    build_one_hot(slot, selector)
    loads[3].wait()
    build_toeplitz(noise, toeplitz)
    loads[4].wait()
    for tile in tiles:
        tile.wait_recv()

    high, low = halves(rows_in[...].reshape(SLOT_ALL, PIX).T)
    table[0:PIX, :] = high
    table[PIX : 2 * PIX, :] = low

    for side, block in ((0, 0), (1, BLOCKS - 1)):

        def keep_edge(row, value):
            samples[row, block + 1 : block + 2, :] = value
            edge_out[side, row : row + 1, :] = value

        read_block(block, table, selector, off, keep_edge)
    after = lax.rem(span + 1, N_TM)
    before = lax.rem(span + N_TM - 1, N_TM)
    edges = [
        remote(edge_out.at[1], edge_in.at[0], edge_s.at[0], edge_r.at[0], (group, after)),
        remote(edge_out.at[0], edge_in.at[1], edge_s.at[1], edge_r.at[1], (group, before)),
    ]

    def read_step(block, carry):
        def keep(row, value):
            samples[row, pl.ds(block + 1, 1), :] = value

        read_block(block, table, selector, off, keep)
        return carry

    lax.fori_loop(1, BLOCKS - 1, read_step, 0)
    for edge in edges:
        edge.wait_recv()
    left = jnp.where(span > 0, edge_in[0], 0.0)
    right = jnp.where(span < N_TM - 1, edge_in[1], 0.0)
    for row in range(ROWS):
        samples[row, 0:1, :] = left[row : row + 1, :]
        samples[row, BLOCKS + 1 : BLOCKS + 2, :] = right[row : row + 1, :]
        samples[row, BLOCKS + 2 : BLOCKS + 4, :] = jnp.zeros((2, PIX), F32)

    filter_samples(samples, toeplitz, filtered)
    scatter_samples(filtered, off, selector, spread, total)
    sums_out[...] = (total[:, :PIX] + total[:, PIX:]).reshape(N_DET, SLOTS, PIX)

    backs = []
    for step in range(1, N_DET):
        owner = lax.rem(group + step, N_DET)
        backs.append(remote(sums_out.at[owner], sums_in.at[group], sums_s.at[step], sums_r.at[step], (owner, span)))
    sums_in[group] = sums_out[group]
    for back in backs:
        back.wait_recv()
    high, low = halves(sums_in[...].reshape(SLOT_ALL, PIX))
    both = jnp.dot(pick_cols[...], jnp.concatenate([high, low], axis=1), preferred_element_type=F32)
    image[...] = (both[:, :PIX] + both[:, PIX:]).reshape(N_Y, N_Z, SUB, PIX)

    turns = (1, 2, 3, 0)
    over_y = {}
    for turn in turns:
        far = lax.rem(z + turn, N_Z)
        for step in range(1, N_Y):
            peer = lax.rem(y + step, N_Y)
            over_y[turn, step] = remote(
                image.at[peer, far], part_y.at[y, far], ry_s.at[turn, step], ry_r.at[turn, step], (group, z * N_Y + peer)
            )
    over_z = {}
    for turn in turns:
        far = lax.rem(z + turn, N_Z)
        value = image[y, far]
        for step in range(1, N_Y):
            over_y[turn, step].wait_recv()
            value = value + part_y[lax.rem(y + N_Y - step, N_Y), far]
        sum_y[far] = value
        if turn:
            over_z[turn] = remote(sum_y.at[far], part_z.at[z], rz_s.at[turn], rz_r.at[turn], (group, far * N_Y + y))
    value = sum_y[z]
    for turn in turns[:3]:
        over_z[turn].wait_recv()
        value = value + part_z[lax.rem(z + N_Z - turn, N_Z)]
    whole[y, z] = value

    back_z = {}
    for turn in turns[:3]:
        far = lax.rem(z + turn, N_Z)
        back_z[turn] = remote(whole.at[y, z], whole.at[y, z], gz_s.at[turn], gz_r.at[turn], (group, far * N_Y + y))
    back_y = {}
    for turn in (0, 1, 2, 3):
        far = lax.rem(z + N_Z - turn, N_Z)
        if turn:
            back_z[turn].wait_recv()
        for step in range(1, N_Y):
            peer = lax.rem(y + step, N_Y)
            back_y[turn, step] = remote(
                whole.at[y, far], whole.at[y, far], gy_s.at[turn, step], gy_r.at[turn, step], (group, z * N_Y + peer)
            )
    for copy in back_y.values():
        copy.wait_recv()
    save = pltpu.make_async_copy(whole, out_h, save_sem)
    save.start()
    sent = requests + tiles + edges + backs
    for copies in (over_y, over_z, back_z, back_y):
        sent += list(copies.values())
    for copy in sent:
        copy.wait_send()
    save.wait()


def on_device(sky_map, tile_slot, pixel_offset, tile_list, noise_kernel):
    anywhere = pl.BlockSpec(memory_space=pl.ANY)
    dma = pltpu.SemaphoreType.DMA
    vmem = pltpu.VMEM
    result = pl.pallas_call(
        kernel,
        out_shape=jax.ShapeDtypeStruct((N_Y, N_Z, SUB, PIX), F32),
        in_specs=[anywhere] * 5,
        out_specs=anywhere,
        scratch_shapes=[
            vmem((TILES, PIX), F32),
            vmem((ROWS, LENGTH), I32),
            vmem((ROWS, LENGTH), I32),
            vmem((1, 1, N_DET, SLOTS), I32),
            vmem((ROWS, W + 1), F32),
            vmem((N_DET, 8, PIX), I32),
            vmem((N_DET, 8, PIX), I32),
            vmem((N_DET, SLOTS, PIX), F32),
            vmem((N_DET, SLOTS, PIX), F32),
            vmem((2, ROWS, PIX), F32),
            vmem((2, ROWS, PIX), F32),
            vmem((N_DET, SLOTS, PIX), F32),
            vmem((N_DET, SLOTS, PIX), F32),
            vmem((TILES, 2 * PIX), BF16),
            vmem((SLOT_ALL, TILES), BF16),
            vmem((TILES, SLOT_ALL), BF16),
            vmem((N_Y, N_Z, SUB, PIX), F32),
            vmem((N_Y, N_Z, SUB, PIX), F32),
            vmem((N_Z, SUB, PIX), F32),
            vmem((N_Z, SUB, PIX), F32),
            vmem((N_Y, N_Z, SUB, PIX), F32),
            vmem((ROWS, 2 * PIX, 2 * PIX), BF16),
            vmem((BLOCKS, SLOT_ALL, WIDE), BF16),
            vmem((2 * PIX, SLOT_ALL), BF16),
            vmem((ROWS, 16, PIX), F32),
            vmem((ROWS, 16, PIX), F32),
            vmem((2 * PIX, WIDE), BF16),
            vmem((SLOT_ALL, 2 * PIX), F32),
            dma((5,)),
            dma((N_DET,)),
            dma((N_DET,)),
            dma((N_DET,)),
            dma((N_DET,)),
            dma((2,)),
            dma((2,)),
            dma((N_DET,)),
            dma((N_DET,)),
            dma((N_Z, N_Y)),
            dma((N_Z, N_Y)),
            dma((N_Z,)),
            dma((N_Z,)),
            dma((N_Z, N_Y)),
            dma((N_Z, N_Y)),
            dma((N_Z,)),
            dma((N_Z,)),
            dma,
        ],
        compiler_params=pltpu.CompilerParams(
            collective_id=0, has_side_effects=True, vmem_limit_bytes=56 * 1024 * 1024
        ),
    )(sky_map, tile_slot, pixel_offset, tile_list, noise_kernel)
    return result.reshape(TILES, PIX)


def solution(mesh):
    return jax.shard_map(
        on_device,
        mesh=mesh,
        in_specs=(
            P("det", None),
            P("det", "tm"),
            P("det", "tm"),
            P("det", "tm", None, None),
            P("det", None),
        ),
        out_specs=P("det", None),
        check_vma=False,
    )
```

time: 694 us -> 75.3 us (0.11)
  waiting for transfers between devices: 331 us -> 0 us
  local copies, waits for them, and re-layouts: 255 us -> 1.87 us
  matrix products: 85.8 us -> 0 us
  Pallas kernels: 0 us -> 72.7 us
  between operations: 13.3 us -> 0.01 us
    gather x5 -> x0, local copies, waits for them, and re-layouts: 240 us -> none  [the longest x4 236 us: filter_rows(): jnp.take(noise_kernel, jnp.minimum(distance, W), axis=1)]
    psum x1 -> x0, waiting for transfers between devices: 170 us -> none  [on_device(): return lax.psum(partial_value, 'tm')]
    reduce_scatter x1 -> x0, waiting for transfers between devices: 101 us -> none  [on_device(): lax.psum_scatter(wide_sums, 'det', scatter_dimension=0, tiled=True)]
    dot_general x26 -> x0, matrix products: 85.8 us -> none  [the longest x12 51.7 us: add_one_block(): lax.dot_general(selector, spread, (((0,), (0,)), ((), ())), precision=lax...]
    pallas_call x0 -> x1, Pallas kernels: none -> 72.7 us  [on_device(): pl.pallas_call(kernel, out_shape=jax.ShapeDtypeStruct((N_Y, N_Z, SUB, PIX...]
    all_gather x1 -> x0, waiting for transfers between devices: 55.5 us -> none  [on_device(): whole = lax.all_gather(sky_map, 'det', axis=0, tiled=True)]
  transfers between devices with their start and end apart: 5 -> 0, of which waited for: 4 -> 0; matrix products, arithmetic and copies ran while one was open for 1% -> 0% of each run, Pallas kernels for 0% -> 0%
where the time goes in v1:
time: 75.3 us; the launch traced here: 74.5 us
  Pallas kernels  72.7 us (97%)
  local copies, waits for them, and re-layouts  1.87 us (2%)
    pallas_call x1, Pallas kernels, on_device(): pl.pallas_call(kernel, out_shape=jax.ShapeDtypeStruct((N_Y, N_Z, SUB, PIX...  72.7 us
    unnamed x1, local copies, waits for them, and re-layouts  1.87 us

profile of v1, /device:TPU:32, one launch (start us, length us, event | category | flops | bytes accessed | tf_op | source)
XLA Modules:
  0.0 74.5 jit_solution(11442807485259859185)
XLA Ops:
  0.0 72.7 %shard_map.55 = f32[4,4,64,128]{3,2,1,0:T(8,128)} custom-call(f32[1024,128]{1,0:T(8,128)} %sky_h.1, s32[16,1536]{1,0:T(8,128)} %slot_h.1, s32[16,1536]{1,0:T(8,128)} %off_h.1, s32[1,1,16,32]{3,2,1,0:T(8,128)} %list_h.1, f32[16,65]{1,0:T(8,128)} %noise_h.1), custom_call_target="tpu_custom_call" | custom-call | tf_op jit(solution)/shard_map/pallas_call | solution.py:305
  72.7 1.9 %copy.7 = f32[1024,128]{1,0:T(8,128)} copy(f32[1024,128]{1,0:T(8,128)} %bitcast.1) | data formatting | bytes 1048576

commit v2 on v1

--- a/solution.py
+++ b/solution.py
@@ -57,7 +57,7 @@
         toeplitz[row, PIX : 2 * PIX, :] = low
 
 
-def build_one_hot(slot, selector):
+def build_one_hot(slot, selector, first, last):
     rank = iota((SLOT_ALL, PIX), 0)
 
     def step(block, carry):
@@ -66,16 +66,16 @@
             selector[block, :, row * PIX : (row + 1) * PIX] = one_hot(rank == slot[row : row + 1, span])
         return carry
 
-    lax.fori_loop(0, BLOCKS, step, 0)
+    lax.fori_loop(first, last, step, 0)
 
 
 def read_block(block, table, selector, off, store):
     rank = iota((PIX, PIX), 0)
     span = pl.ds(pl.multiple_of(block * PIX, PIX), PIX)
-    for row in range(0, ROWS, 2):
-        both = jnp.dot(table[...], selector[block, :, row * PIX : (row + 2) * PIX], preferred_element_type=F32)
+    for row in range(0, ROWS, 4):
+        both = jnp.dot(table[...], selector[block, :, row * PIX : (row + 4) * PIX], preferred_element_type=F32)
         both = both[:PIX] + both[PIX:]
-        for more in range(2):
+        for more in range(4):
             mask = rank == off[row + more : row + more + 1, span]
             part = both[:, more * PIX : (more + 1) * PIX]
             store(row + more, jnp.sum(jnp.where(mask, part, 0.0), axis=0, keepdims=True))
@@ -92,33 +92,34 @@
         filtered[row] = out[:16, :PIX] + out[:16, PIX:] + out[16:, :PIX]
 
 
-def scatter_samples(filtered, off, selector, spread, total):
+def scatter_samples(filtered, off, selector, total):
     rank = iota((PIX, PIX), 0)
     total[...] = jnp.zeros_like(total)
 
     def step(block, carry):
         span = pl.ds(pl.multiple_of(block * PIX, PIX), PIX)
+        highs, lows = [], []
         for row in range(ROWS):
             mask = rank == off[row : row + 1, span]
             value = filtered[row, pl.ds(block, 1), :]
             high = value.astype(BF16).astype(F32)
-            cols = slice(row * PIX, (row + 1) * PIX)
-            spread[0:PIX, cols] = jnp.where(mask, high, 0.0).astype(BF16)
-            spread[PIX : 2 * PIX, cols] = jnp.where(mask, value - high, 0.0).astype(BF16)
-        total[...] += lax.dot_general(selector[block], spread[...], NT, preferred_element_type=F32)
+            highs.append(jnp.where(mask, high, 0.0).astype(BF16))
+            lows.append(jnp.where(mask, value - high, 0.0).astype(BF16))
+        spread = jnp.concatenate([jnp.concatenate(highs, axis=1), jnp.concatenate(lows, axis=1)], axis=0)
+        total[...] += lax.dot_general(selector[block], spread, NT, preferred_element_type=F32)
         return carry
 
-    lax.fori_loop(0, BLOCKS, step, 0)
+    lax.fori_loop(0, BLOCKS, step, 0, unroll=4)
 
 
 def kernel(
-    sky_h, slot_h, off_h, list_h, noise_h, out_h,
+    sky_h, slot_h, off_h, list_h, noise_h, whole,
     sky, slot, off, wanted, noise,
     req_out, req_in, rows_out, rows_in, edge_out, edge_in, sums_out, sums_in,
-    sky_parts, pick_rows, pick_cols, image, part_y, sum_y, part_z, whole,
-    toeplitz, selector, table, samples, filtered, spread, total,
+    sky_parts, pick_rows, pick_cols, image, part_y, sum_y, part_z,
+    toeplitz, selector, table, samples, filtered, total,
     load_sem, req_s, req_r, rows_s, rows_r, edge_s, edge_r, sums_s, sums_r,
-    ry_s, ry_r, rz_s, rz_r, gy_s, gy_r, gz_s, gz_r, save_sem,
+    ry_s, ry_r, rz_s, rz_r, gy_s, gy_r, gz_s, gz_r,
 ):
     group = lax.axis_index("det")
     span = lax.axis_index("tm")
@@ -165,6 +166,8 @@
     high, low = halves(sky[...])
     sky_parts[:, 0:PIX] = high
     sky_parts[:, PIX : 2 * PIX] = low
+    loads[2].wait()
+    build_one_hot(slot, selector, 0, BLOCKS // 2)
     for request in requests:
         request.wait_recv()
 
@@ -189,8 +192,7 @@
 
     for four in range(4):
         pick_cols[:, four * PIX : (four + 1) * PIX] = one_hot(iota((TILES, PIX), 0) == lists[four])
-    loads[2].wait()
-    build_one_hot(slot, selector)
+    build_one_hot(slot, selector, BLOCKS // 2, BLOCKS)
     loads[3].wait()
     build_toeplitz(noise, toeplitz)
     loads[4].wait()
@@ -222,7 +224,7 @@
         read_block(block, table, selector, off, keep)
         return carry
 
-    lax.fori_loop(1, BLOCKS - 1, read_step, 0)
+    lax.fori_loop(1, BLOCKS - 1, read_step, 0, unroll=5)
     for edge in edges:
         edge.wait_recv()
     left = jnp.where(span > 0, edge_in[0], 0.0)
@@ -233,7 +235,7 @@
         samples[row, BLOCKS + 2 : BLOCKS + 4, :] = jnp.zeros((2, PIX), F32)
 
     filter_samples(samples, toeplitz, filtered)
-    scatter_samples(filtered, off, selector, spread, total)
+    scatter_samples(filtered, off, selector, total)
     sums_out[...] = (total[:, :PIX] + total[:, PIX:]).reshape(N_DET, SLOTS, PIX)
 
     backs = []
@@ -288,25 +290,22 @@
             )
     for copy in back_y.values():
         copy.wait_recv()
-    save = pltpu.make_async_copy(whole, out_h, save_sem)
-    save.start()
     sent = requests + tiles + edges + backs
     for copies in (over_y, over_z, back_z, back_y):
         sent += list(copies.values())
     for copy in sent:
         copy.wait_send()
-    save.wait()
 
 
 def on_device(sky_map, tile_slot, pixel_offset, tile_list, noise_kernel):
-    anywhere = pl.BlockSpec(memory_space=pl.ANY)
+    far = pl.BlockSpec(memory_space=pltpu.HBM)
     dma = pltpu.SemaphoreType.DMA
     vmem = pltpu.VMEM
     result = pl.pallas_call(
         kernel,
-        out_shape=jax.ShapeDtypeStruct((N_Y, N_Z, SUB, PIX), F32),
-        in_specs=[anywhere] * 5,
-        out_specs=anywhere,
+        out_shape=vmem((N_Y, N_Z, SUB, PIX), F32),
+        in_specs=[far] * 5,
+        out_specs=pl.BlockSpec(memory_space=vmem),
         scratch_shapes=[
             vmem((TILES, PIX), F32),
             vmem((ROWS, LENGTH), I32),
@@ -328,13 +327,11 @@
             vmem((N_Y, N_Z, SUB, PIX), F32),
             vmem((N_Z, SUB, PIX), F32),
             vmem((N_Z, SUB, PIX), F32),
-            vmem((N_Y, N_Z, SUB, PIX), F32),
             vmem((ROWS, 2 * PIX, 2 * PIX), BF16),
             vmem((BLOCKS, SLOT_ALL, WIDE), BF16),
             vmem((2 * PIX, SLOT_ALL), BF16),
             vmem((ROWS, 16, PIX), F32),
             vmem((ROWS, 16, PIX), F32),
-            vmem((2 * PIX, WIDE), BF16),
             vmem((SLOT_ALL, 2 * PIX), F32),
             dma((5,)),
             dma((N_DET,)),
@@ -353,7 +350,6 @@
             dma((N_Z, N_Y)),
             dma((N_Z,)),
             dma((N_Z,)),
-            dma,
         ],
         compiler_params=pltpu.CompilerParams(
             collective_id=0, has_side_effects=True, vmem_limit_bytes=56 * 1024 * 1024

time: 75.3 us -> 66.5 us (0.88)
  Pallas kernels: 72.7 us -> 65.6 us
  local copies, waits for them, and re-layouts: 1.87 us -> 0.8 us
    pallas_call x1, Pallas kernels: 72.7 us -> 65.6 us  [on_device(): pl.pallas_call(kernel, out_shape=vmem((N_Y, N_Z, SUB, PIX), F32), in_spec...]
    unnamed x1, local copies, waits for them, and re-layouts: 1.87 us -> 0.8 us
where the time goes in v2:
time: 66.5 us; the launch traced here: 66.4 us
  Pallas kernels  65.6 us (99%)
  local copies, waits for them, and re-layouts  0.8 us (1%)
    pallas_call x1, Pallas kernels, on_device(): pl.pallas_call(kernel, out_shape=vmem((N_Y, N_Z, SUB, PIX), F32), in_spec...  65.6 us

profile of v2, /device:TPU:32, one launch (start us, length us, event | category | flops | bytes accessed | tf_op | source)
XLA Modules:
  0.0 66.4 jit_solution(16003145739445937226)
XLA Ops:
  0.0 65.6 %shard_map.55 = f32[4,4,64,128]{3,2,1,0:T(8,128)S(1)} custom-call(f32[1024,128]{1,0:T(8,128)} %sky_h.1, s32[16,1536]{1,0:T(8,128)} %slot_h.1, s32[16,1536]{1,0:T(8,128)} %off_h.1, s32[1,1,16,32]{3,2,1,0:T(8,128)} %list_h.1, f32[16,65]{1,0:T(8,128)} %noise_h.1), custom_call_target="tpu_custom_call" | custom-call | tf_op jit(solution)/shard_map/pallas_call | solution.py:304
  65.6 0.8 %copy.7 = f32[1024,128]{1,0:T(8,128)} copy(f32[1024,128]{1,0:T(8,128)S(1)} %bitcast.1) | data formatting | bytes 1048576

commit v3 on v2

--- a/solution.py
+++ b/solution.py
@@ -18,6 +18,8 @@
 SLOTS = 32
 SLOT_ALL = N_DET * SLOTS
 SUB = TILES // (N_Y * N_Z)
+PART = PIX // N_Y
+FAR_FIRST = (8, 9, 7, 10, 6, 11, 5, 12, 4, 13, 3, 14, 2, 15, 1)
 WIDE = ROWS * PIX
 
 F32 = jnp.float32
@@ -92,6 +94,19 @@
         filtered[row] = out[:16, :PIX] + out[:16, PIX:] + out[16:, :PIX]
 
 
+def lane_part():
+    return lax.div(iota((1, PIX), 1), PART)
+
+
+def turn_parts(values, shifts):
+    result = None
+    for place, (value, shift) in enumerate(zip(values, shifts)):
+        shift = shift % N_Y * PART
+        moved = pltpu.roll(value, shift, 1) if shift else value
+        result = moved if result is None else jnp.where(lane_part() == place, moved, result)
+    return result
+
+
 def scatter_samples(filtered, off, selector, total):
     rank = iota((PIX, PIX), 0)
     total[...] = jnp.zeros_like(total)
@@ -114,12 +129,12 @@
 
 def kernel(
     sky_h, slot_h, off_h, list_h, noise_h, whole,
-    sky, slot, off, wanted, noise,
-    req_out, req_in, rows_out, rows_in, edge_out, edge_in, sums_out, sums_in,
-    sky_parts, pick_rows, pick_cols, image, part_y, sum_y, part_z,
+    sky, slot, off, noise,
+    req_in, list_in, pick_in, rows_out, rows_in, edge_out, edge_in, sums_out, sums_in,
+    sky_parts, pick_rows, pick_cols, image, part_z, packed,
     toeplitz, selector, table, samples, filtered, total,
-    load_sem, req_s, req_r, rows_s, rows_r, edge_s, edge_r, sums_s, sums_r,
-    ry_s, ry_r, rz_s, rz_r, gy_s, gy_r, gz_s, gz_r,
+    load_sem, req_s, req_r, pick_s, pick_r, rows_s, rows_r, edge_s, edge_r, sums_s, sums_r,
+    rz_s, rz_r, gy_s, gy_r, gz_s, gz_r,
 ):
     group = lax.axis_index("det")
     span = lax.axis_index("tm")
@@ -134,9 +149,7 @@
 
     loads = [
         pltpu.make_async_copy(source, target, load_sem.at[number])
-        for number, (source, target) in enumerate(
-            [(list_h, wanted), (sky_h, sky), (slot_h, slot), (noise_h, noise), (off_h, off)]
-        )
+        for number, (source, target) in enumerate([(list_h.at[0, 0], req_in.at[group]), (sky_h, sky), (slot_h, slot), (noise_h, noise), (off_h, off)])
     ]
     for load in loads:
         load.start()
@@ -148,19 +161,11 @@
         copy.start()
         return copy
 
-    sent = []
-
-    loads[0].wait()
-    mine = wanted[0, 0]
-    mine = jnp.concatenate([mine] * (PIX // SLOTS), axis=1)
-    for owner in range(N_DET):
-        req_out[owner] = jnp.broadcast_to(mine[owner : owner + 1, :], (8, PIX))
     pl.semaphore_wait(barrier, N_DET + N_TM - 2)
     requests = []
-    for step in range(1, N_DET):
+    for step in FAR_FIRST:
         owner = lax.rem(group + step, N_DET)
-        requests.append(remote(req_out.at[owner], req_in.at[group], req_s.at[step], req_r.at[step], (owner, span)))
-    req_in[group] = req_out[group]
+        requests.append(remote(list_h.at[0, 0], req_in.at[group], req_s.at[step], req_r.at[step], (owner, span)))
 
     loads[1].wait()
     high, low = halves(sky[...])
@@ -168,30 +173,38 @@
     sky_parts[:, PIX : 2 * PIX] = low
     loads[2].wait()
     build_one_hot(slot, selector, 0, BLOCKS // 2)
+    loads[0].wait()
     for request in requests:
         request.wait_recv()
 
-    lane = iota((1, PIX), 1)
-    lists = []
-    for four in range(4):
-        row = req_in[4 * four, 0:1, :]
-        for place in range(1, 4):
-            row = jnp.where(lane >= place * SLOTS, req_in[4 * four + place, 0:1, :], row)
-        lists.append(row)
-    upright = jnp.concatenate(lists + [jnp.zeros((4, PIX), I32)], axis=0).T
-    for four in range(4):
-        chosen = upright[:, four : four + 1] == iota((PIX, TILES), 1)
-        pick_rows[four * PIX : (four + 1) * PIX, :] = one_hot(chosen)
+    for peer in range(N_DET):
+        list_in[peer : peer + 1, 0:SLOTS] = req_in[peer, pl.ds(group, 1), :]
+    lists = list_in[:, 0:SLOTS]
+    lists = jnp.concatenate([lists] * (PIX // SLOTS), axis=1)
+    upright = lists.T
+    for peer in range(N_DET):
+        chosen = upright[0:SLOTS, peer : peer + 1] == iota((SLOTS, TILES), 1)
+        pick_rows[peer * SLOTS : (peer + 1) * SLOTS, :] = one_hot(chosen)
     both = jnp.dot(pick_rows[...], sky_parts[...], preferred_element_type=F32)
     rows_out[...] = (both[:, :PIX] + both[:, PIX:]).reshape(N_DET, SLOTS, PIX)
     tiles = []
-    for step in range(1, N_DET):
+    for step in FAR_FIRST:
         reader = lax.rem(group + step, N_DET)
         tiles.append(remote(rows_out.at[reader], rows_in.at[group], rows_s.at[step], rows_r.at[step], (reader, span)))
     rows_in[group] = rows_out[group]
 
-    for four in range(4):
-        pick_cols[:, four * PIX : (four + 1) * PIX] = one_hot(iota((TILES, PIX), 0) == lists[four])
+    for peer in range(N_DET):
+        list_in[peer : peer + 1, :] = pltpu.roll(lists[peer : peer + 1, :], 8 * peer, 1) if peer else lists[0:1, :]
+    own_lane = lax.div(iota((N_DET, PIX), 1), 8) == iota((N_DET, PIX), 0)
+    for place in range(N_Y):
+        turned = pltpu.roll(list_in[...], PIX - 8 * place, 1) if place else list_in[...]
+        pick_in[y, place : place + 1, :] = jnp.sum(jnp.where(own_lane, turned, 0), axis=0, keepdims=True)
+    pick_in[y, N_Y : 2 * N_Y, :] = jnp.zeros((N_Y, PIX), I32)
+    picks = []
+    for step in (2, 1, 3):
+        peer = lax.rem(y + step, N_Y)
+        picks.append(remote(pick_in.at[y], pick_in.at[y], pick_s.at[step], pick_r.at[step], (group, z * N_Y + peer)))
+
     build_one_hot(slot, selector, BLOCKS // 2, BLOCKS)
     loads[3].wait()
     build_toeplitz(noise, toeplitz)
@@ -236,62 +249,76 @@
 
     filter_samples(samples, toeplitz, filtered)
     scatter_samples(filtered, off, selector, total)
-    sums_out[...] = (total[:, :PIX] + total[:, PIX:]).reshape(N_DET, SLOTS, PIX)
-
+    sums = (total[:, :PIX] + total[:, PIX:]).reshape(N_DET, N_Y, 8, PIX)
+    places = [sums[:, place].reshape(N_DET * 8, PIX) for place in range(N_Y)]
+    for part in range(N_Y):
+        sums_out[part] = turn_parts(places, [place - part for place in range(N_Y)]).reshape(N_DET, 8, PIX)
+
+    for pick in picks:
+        pick.wait_recv()
     backs = []
-    for step in range(1, N_DET):
+    for step in FAR_FIRST + (0,):
         owner = lax.rem(group + step, N_DET)
-        backs.append(remote(sums_out.at[owner], sums_in.at[group], sums_s.at[step], sums_r.at[step], (owner, span)))
-    sums_in[group] = sums_out[group]
+        for more in (2, 1, 3, 0):
+            if step or more:
+                part = lax.rem(y + more, N_Y)
+                backs.append(
+                    remote(
+                        sums_out.at[part, owner], sums_in.at[y, group],
+                        sums_s.at[more, step], sums_r.at[more, step], (owner, z * N_Y + part),
+                    )
+                )
+    sums_in[y, group] = sums_out[y, group]
+    for place in range(N_Y):
+        for peer in range(N_Y):
+            start = (place * N_Y + peer) * PIX
+            pick_cols[:, start : start + PIX] = one_hot(iota((TILES, PIX), 0) == pick_in[peer, place : place + 1, :])
     for back in backs:
         back.wait_recv()
-    high, low = halves(sums_in[...].reshape(SLOT_ALL, PIX))
+    came = sums_in[...].reshape(N_Y * N_DET * 8, PIX)
+    came = jnp.concatenate([jnp.where(lane_part() == place, came, 0.0) for place in range(N_Y)], axis=0)
+    high, low = halves(came)
     both = jnp.dot(pick_cols[...], jnp.concatenate([high, low], axis=1), preferred_element_type=F32)
-    image[...] = (both[:, :PIX] + both[:, PIX:]).reshape(N_Y, N_Z, SUB, PIX)
-
-    turns = (1, 2, 3, 0)
-    over_y = {}
-    for turn in turns:
+    both = both[:, :PIX] + both[:, PIX:]
+    both = both + pltpu.roll(both, 2 * PART, 1)
+    both = both + pltpu.roll(both, PART, 1)
+    both = both.reshape(N_Z, N_Y, SUB, PIX)
+    for far in range(N_Z):
+        image[far] = turn_parts([both[far, place] for place in range(N_Y)], [0] * N_Y)
+
+    over_z = {}
+    for turn in (2, 1, 3):
         far = lax.rem(z + turn, N_Z)
-        for step in range(1, N_Y):
-            peer = lax.rem(y + step, N_Y)
-            over_y[turn, step] = remote(
-                image.at[peer, far], part_y.at[y, far], ry_s.at[turn, step], ry_r.at[turn, step], (group, z * N_Y + peer)
-            )
-    over_z = {}
-    for turn in turns:
-        far = lax.rem(z + turn, N_Z)
-        value = image[y, far]
-        for step in range(1, N_Y):
-            over_y[turn, step].wait_recv()
-            value = value + part_y[lax.rem(y + N_Y - step, N_Y), far]
-        sum_y[far] = value
-        if turn:
-            over_z[turn] = remote(sum_y.at[far], part_z.at[z], rz_s.at[turn], rz_r.at[turn], (group, far * N_Y + y))
-    value = sum_y[z]
-    for turn in turns[:3]:
+        over_z[turn] = remote(image.at[far], part_z.at[z], rz_s.at[turn], rz_r.at[turn], (group, far * N_Y + y))
+    value = image[z]
+    for turn in (1, 3, 2):
         over_z[turn].wait_recv()
         value = value + part_z[lax.rem(z + N_Z - turn, N_Z)]
-    whole[y, z] = value
+    packed[y, z] = value
 
     back_z = {}
-    for turn in turns[:3]:
+    for turn in (2, 1, 3):
         far = lax.rem(z + turn, N_Z)
-        back_z[turn] = remote(whole.at[y, z], whole.at[y, z], gz_s.at[turn], gz_r.at[turn], (group, far * N_Y + y))
+        back_z[turn] = remote(packed.at[y, z], packed.at[y, z], gz_s.at[turn], gz_r.at[turn], (group, far * N_Y + y))
     back_y = {}
-    for turn in (0, 1, 2, 3):
+    for turn in (0, 1, 3, 2):
         far = lax.rem(z + N_Z - turn, N_Z)
         if turn:
             back_z[turn].wait_recv()
-        for step in range(1, N_Y):
+        for step in (2, 1, 3):
             peer = lax.rem(y + step, N_Y)
             back_y[turn, step] = remote(
-                whole.at[y, far], whole.at[y, far], gy_s.at[turn, step], gy_r.at[turn, step], (group, z * N_Y + peer)
+                packed.at[y, far], packed.at[y, far], gy_s.at[turn, step], gy_r.at[turn, step], (group, z * N_Y + peer)
             )
-    for copy in back_y.values():
-        copy.wait_recv()
-    sent = requests + tiles + edges + backs
-    for copies in (over_y, over_z, back_z, back_y):
+    for turn in (0, 1, 3, 2):
+        far = lax.rem(z + N_Z - turn, N_Z)
+        for step in (1, 3, 2):
+            back_y[turn, step].wait_recv()
+        parts = [packed[part, far] for part in range(N_Y)]
+        for place in range(N_Y):
+            whole[far, place] = turn_parts(parts, [part - place for part in range(N_Y)])
+    sent = requests + picks + tiles + edges + backs
+    for copies in (over_z, back_z, back_y):
         sent += list(copies.values())
     for copy in sent:
         copy.wait_send()
@@ -310,23 +337,22 @@
             vmem((TILES, PIX), F32),
             vmem((ROWS, LENGTH), I32),
             vmem((ROWS, LENGTH), I32),
-            vmem((1, 1, N_DET, SLOTS), I32),
             vmem((ROWS, W + 1), F32),
-            vmem((N_DET, 8, PIX), I32),
-            vmem((N_DET, 8, PIX), I32),
+            vmem((N_DET, N_DET, SLOTS), I32),
+            vmem((N_DET, PIX), I32),
+            vmem((N_Y, 8, PIX), I32),
             vmem((N_DET, SLOTS, PIX), F32),
             vmem((N_DET, SLOTS, PIX), F32),
             vmem((2, ROWS, PIX), F32),
             vmem((2, ROWS, PIX), F32),
-            vmem((N_DET, SLOTS, PIX), F32),
-            vmem((N_DET, SLOTS, PIX), F32),
+            vmem((N_Y, N_DET, 8, PIX), F32),
+            vmem((N_Y, N_DET, 8, PIX), F32),
             vmem((TILES, 2 * PIX), BF16),
             vmem((SLOT_ALL, TILES), BF16),
-            vmem((TILES, SLOT_ALL), BF16),
-            vmem((N_Y, N_Z, SUB, PIX), F32),
-            vmem((N_Y, N_Z, SUB, PIX), F32),
+            vmem((TILES, N_Y * SLOT_ALL), BF16),
             vmem((N_Z, SUB, PIX), F32),
             vmem((N_Z, SUB, PIX), F32),
+            vmem((N_Y, N_Z, SUB, PIX), F32),
             vmem((ROWS, 2 * PIX, 2 * PIX), BF16),
             vmem((BLOCKS, SLOT_ALL, WIDE), BF16),
             vmem((2 * PIX, SLOT_ALL), BF16),
@@ -336,14 +362,14 @@
             dma((5,)),
             dma((N_DET,)),
             dma((N_DET,)),
+            dma((N_Y,)),
+            dma((N_Y,)),
             dma((N_DET,)),
             dma((N_DET,)),
             dma((2,)),
             dma((2,)),
-            dma((N_DET,)),
-            dma((N_DET,)),
-            dma((N_Z, N_Y)),
-            dma((N_Z, N_Y)),
+            dma((N_Y, N_DET)),
+            dma((N_Y, N_DET)),
             dma((N_Z,)),
             dma((N_Z,)),
             dma((N_Z, N_Y)),

time: 66.5 us -> 64.5 us (0.970)
  the two profiles are of different devices: /device:TPU:32 before, /device:TPU:8 now
where the time goes in v3:
time: 64.5 us
  Pallas kernels  63.6 us (99%)
  local copies, waits for them, and re-layouts  0.8 us (1%)
    pallas_call x1, Pallas kernels, on_device(): pl.pallas_call(kernel, out_shape=vmem((N_Y, N_Z, SUB, PIX), F32), in_spec...  63.6 us

profile of v3, /device:TPU:8, one launch (start us, length us, event | category | flops | bytes accessed | tf_op | source)
XLA Modules:
  0.0 64.5 jit_solution(13780429908765572766)
XLA Ops:
  0.0 63.6 %shard_map.55 = f32[4,4,64,128]{3,2,1,0:T(8,128)S(1)} custom-call(f32[1024,128]{1,0:T(8,128)} %sky_h.1, s32[16,1536]{1,0:T(8,128)} %slot_h.1, s32[16,1536]{1,0:T(8,128)} %off_h.1, s32[1,1,16,32]{3,2,1,0:T(8,128)} %list_h.1, f32[16,65]{1,0:T(8,128)} %noise_h.1), custom_call_target="tpu_custom_call" | custom-call | tf_op jit(solution)/shard_map/pallas_call | solution.py:331
  63.7 0.8 %copy.7 = f32[1024,128]{1,0:T(8,128)} copy(f32[1024,128]{1,0:T(8,128)S(1)} %bitcast.1) | data formatting | bytes 1048576

commit v4 on v3

--- a/solution.py
+++ b/solution.py
@@ -134,7 +134,7 @@
     sky_parts, pick_rows, pick_cols, image, part_z, packed,
     toeplitz, selector, table, samples, filtered, total,
     load_sem, req_s, req_r, pick_s, pick_r, rows_s, rows_r, edge_s, edge_r, sums_s, sums_r,
-    rz_s, rz_r, gy_s, gy_r, gz_s, gz_r,
+    rz_s, rz_r, gz_s, gz_r, gy_s, gy_r,
 ):
     group = lax.axis_index("det")
     span = lax.axis_index("tm")
@@ -144,8 +144,22 @@
     barrier = pltpu.get_barrier_semaphore()
     for step in range(1, N_DET):
         pl.semaphore_signal(barrier, inc=1, device_id=(lax.rem(group + step, N_DET), span), device_id_type=MESH)
-    for step in range(1, N_TM):
-        pl.semaphore_signal(barrier, inc=1, device_id=(group, lax.rem(span + step, N_TM)), device_id_type=MESH)
+    for step in range(1, N_Y):
+        pl.semaphore_signal(barrier, inc=1, device_id=(group, z * N_Y + lax.rem(y + step, N_Y)), device_id_type=MESH)
+    for step in range(1, N_Z):
+        pl.semaphore_signal(barrier, inc=1, device_id=(group, lax.rem(z + step, N_Z) * N_Y + y), device_id_type=MESH)
+    after = lax.rem(span + 1, N_TM)
+    before = lax.rem(span + N_TM - 1, N_TM)
+
+    @pl.when(y == N_Y - 1)
+    def greet_after():
+        pl.semaphore_signal(barrier, inc=1, device_id=(group, after), device_id_type=MESH)
+
+    @pl.when(y == 0)
+    def greet_before():
+        pl.semaphore_signal(barrier, inc=1, device_id=(group, before), device_id_type=MESH)
+
+    greeted = N_DET + N_Y + N_Z - 3 + lax.rem(lax.div(y + 1, 2) + 1, 2)
 
     loads = [
         pltpu.make_async_copy(source, target, load_sem.at[number])
@@ -154,18 +168,24 @@
     for load in loads:
         load.start()
 
-    def remote(source, target, send, recv, device):
-        copy = pltpu.make_async_remote_copy(
+    def descriptor(source, target, send, recv, device):
+        return pltpu.make_async_remote_copy(
             src_ref=source, dst_ref=target, send_sem=send, recv_sem=recv, device_id=device, device_id_type=MESH
         )
-        copy.start()
-        return copy
-
-    pl.semaphore_wait(barrier, N_DET + N_TM - 2)
-    requests = []
+
+    def remote(source, target, send, recv, device):
+        descriptor(source, target, send, recv, device).start()
+
+    def came(buffer, recv):
+        descriptor(buffer, buffer, recv, recv, (group, span)).wait_recv()
+
+    def left(buffer, send):
+        descriptor(buffer, buffer, send, send, (group, span)).wait_send()
+
+    pl.semaphore_wait(barrier, greeted)
     for step in FAR_FIRST:
         owner = lax.rem(group + step, N_DET)
-        requests.append(remote(list_h.at[0, 0], req_in.at[group], req_s.at[step], req_r.at[step], (owner, span)))
+        remote(list_h.at[0, 0], req_in.at[group], req_s, req_r, (owner, span))
 
     loads[1].wait()
     high, low = halves(sky[...])
@@ -174,8 +194,7 @@
     loads[2].wait()
     build_one_hot(slot, selector, 0, BLOCKS // 2)
     loads[0].wait()
-    for request in requests:
-        request.wait_recv()
+    came(req_in.at[0 : N_DET - 1], req_r)
 
     for peer in range(N_DET):
         list_in[peer : peer + 1, 0:SLOTS] = req_in[peer, pl.ds(group, 1), :]
@@ -187,10 +206,9 @@
         pick_rows[peer * SLOTS : (peer + 1) * SLOTS, :] = one_hot(chosen)
     both = jnp.dot(pick_rows[...], sky_parts[...], preferred_element_type=F32)
     rows_out[...] = (both[:, :PIX] + both[:, PIX:]).reshape(N_DET, SLOTS, PIX)
-    tiles = []
     for step in FAR_FIRST:
         reader = lax.rem(group + step, N_DET)
-        tiles.append(remote(rows_out.at[reader], rows_in.at[group], rows_s.at[step], rows_r.at[step], (reader, span)))
+        remote(rows_out.at[reader], rows_in.at[group], rows_s, rows_r, (reader, span))
     rows_in[group] = rows_out[group]
 
     for peer in range(N_DET):
@@ -200,17 +218,15 @@
         turned = pltpu.roll(list_in[...], PIX - 8 * place, 1) if place else list_in[...]
         pick_in[y, place : place + 1, :] = jnp.sum(jnp.where(own_lane, turned, 0), axis=0, keepdims=True)
     pick_in[y, N_Y : 2 * N_Y, :] = jnp.zeros((N_Y, PIX), I32)
-    picks = []
     for step in (2, 1, 3):
         peer = lax.rem(y + step, N_Y)
-        picks.append(remote(pick_in.at[y], pick_in.at[y], pick_s.at[step], pick_r.at[step], (group, z * N_Y + peer)))
+        remote(pick_in.at[y], pick_in.at[y], pick_s, pick_r, (group, z * N_Y + peer))
 
     build_one_hot(slot, selector, BLOCKS // 2, BLOCKS)
     loads[3].wait()
     build_toeplitz(noise, toeplitz)
     loads[4].wait()
-    for tile in tiles:
-        tile.wait_recv()
+    came(rows_in.at[0 : N_DET - 1], rows_r)
 
     high, low = halves(rows_in[...].reshape(SLOT_ALL, PIX).T)
     table[0:PIX, :] = high
@@ -223,12 +239,8 @@
             edge_out[side, row : row + 1, :] = value
 
         read_block(block, table, selector, off, keep_edge)
-    after = lax.rem(span + 1, N_TM)
-    before = lax.rem(span + N_TM - 1, N_TM)
-    edges = [
-        remote(edge_out.at[1], edge_in.at[0], edge_s.at[0], edge_r.at[0], (group, after)),
-        remote(edge_out.at[0], edge_in.at[1], edge_s.at[1], edge_r.at[1], (group, before)),
-    ]
+    remote(edge_out.at[1], edge_in.at[0], edge_s, edge_r, (group, after))
+    remote(edge_out.at[0], edge_in.at[1], edge_s, edge_r, (group, before))
 
     def read_step(block, carry):
         def keep(row, value):
@@ -238,13 +250,12 @@
         return carry
 
     lax.fori_loop(1, BLOCKS - 1, read_step, 0, unroll=5)
-    for edge in edges:
-        edge.wait_recv()
-    left = jnp.where(span > 0, edge_in[0], 0.0)
-    right = jnp.where(span < N_TM - 1, edge_in[1], 0.0)
+    came(edge_in, edge_r)
+    first = jnp.where(span > 0, edge_in[0], 0.0)
+    last = jnp.where(span < N_TM - 1, edge_in[1], 0.0)
     for row in range(ROWS):
-        samples[row, 0:1, :] = left[row : row + 1, :]
-        samples[row, BLOCKS + 1 : BLOCKS + 2, :] = right[row : row + 1, :]
+        samples[row, 0:1, :] = first[row : row + 1, :]
+        samples[row, BLOCKS + 1 : BLOCKS + 2, :] = last[row : row + 1, :]
         samples[row, BLOCKS + 2 : BLOCKS + 4, :] = jnp.zeros((2, PIX), F32)
 
     filter_samples(samples, toeplitz, filtered)
@@ -252,32 +263,25 @@
     sums = (total[:, :PIX] + total[:, PIX:]).reshape(N_DET, N_Y, 8, PIX)
     places = [sums[:, place].reshape(N_DET * 8, PIX) for place in range(N_Y)]
     for part in range(N_Y):
-        sums_out[part] = turn_parts(places, [place - part for place in range(N_Y)]).reshape(N_DET, 8, PIX)
-
-    for pick in picks:
-        pick.wait_recv()
-    backs = []
+        turned = turn_parts(places, [place - part for place in range(N_Y)])
+        sums_out[part * N_DET : (part + 1) * N_DET] = turned.reshape(N_DET, 8, PIX)
+
+    came(pick_in.at[0 : N_Y - 1], pick_r)
     for step in FAR_FIRST + (0,):
         owner = lax.rem(group + step, N_DET)
         for more in (2, 1, 3, 0):
             if step or more:
                 part = lax.rem(y + more, N_Y)
-                backs.append(
-                    remote(
-                        sums_out.at[part, owner], sums_in.at[y, group],
-                        sums_s.at[more, step], sums_r.at[more, step], (owner, z * N_Y + part),
-                    )
-                )
-    sums_in[y, group] = sums_out[y, group]
+                remote(sums_out.at[part * N_DET + owner], sums_in.at[y * N_DET + group], sums_s, sums_r, (owner, z * N_Y + part))
+    sums_in[y * N_DET + group] = sums_out[y * N_DET + group]
     for place in range(N_Y):
         for peer in range(N_Y):
             start = (place * N_Y + peer) * PIX
             pick_cols[:, start : start + PIX] = one_hot(iota((TILES, PIX), 0) == pick_in[peer, place : place + 1, :])
-    for back in backs:
-        back.wait_recv()
-    came = sums_in[...].reshape(N_Y * N_DET * 8, PIX)
-    came = jnp.concatenate([jnp.where(lane_part() == place, came, 0.0) for place in range(N_Y)], axis=0)
-    high, low = halves(came)
+    came(sums_in.at[0 : N_Y * N_DET - 1], sums_r)
+    rows = sums_in[...].reshape(N_Y * N_DET * 8, PIX)
+    rows = jnp.concatenate([jnp.where(lane_part() == place, rows, 0.0) for place in range(N_Y)], axis=0)
+    high, low = halves(rows)
     both = jnp.dot(pick_cols[...], jnp.concatenate([high, low], axis=1), preferred_element_type=F32)
     both = both[:, :PIX] + both[:, PIX:]
     both = both + pltpu.roll(both, 2 * PART, 1)
@@ -286,42 +290,39 @@
     for far in range(N_Z):
         image[far] = turn_parts([both[far, place] for place in range(N_Y)], [0] * N_Y)
 
-    over_z = {}
     for turn in (2, 1, 3):
         far = lax.rem(z + turn, N_Z)
-        over_z[turn] = remote(image.at[far], part_z.at[z], rz_s.at[turn], rz_r.at[turn], (group, far * N_Y + y))
+        remote(image.at[far], part_z.at[z], rz_s, rz_r, (group, far * N_Y + y))
+    came(part_z.at[0 : N_Z - 1], rz_r)
     value = image[z]
     for turn in (1, 3, 2):
-        over_z[turn].wait_recv()
         value = value + part_z[lax.rem(z + N_Z - turn, N_Z)]
     packed[y, z] = value
 
-    back_z = {}
     for turn in (2, 1, 3):
         far = lax.rem(z + turn, N_Z)
-        back_z[turn] = remote(packed.at[y, z], packed.at[y, z], gz_s.at[turn], gz_r.at[turn], (group, far * N_Y + y))
-    back_y = {}
+        remote(packed.at[y, z], packed.at[y, z], gz_s, gz_r.at[turn], (group, far * N_Y + y))
     for turn in (0, 1, 3, 2):
         far = lax.rem(z + N_Z - turn, N_Z)
         if turn:
-            back_z[turn].wait_recv()
+            came(packed.at[y, far], gz_r.at[turn])
         for step in (2, 1, 3):
             peer = lax.rem(y + step, N_Y)
-            back_y[turn, step] = remote(
-                packed.at[y, far], packed.at[y, far], gy_s.at[turn, step], gy_r.at[turn, step], (group, z * N_Y + peer)
-            )
+            remote(packed.at[y, far], packed.at[y, far], gy_s, gy_r.at[turn], (group, z * N_Y + peer))
     for turn in (0, 1, 3, 2):
         far = lax.rem(z + N_Z - turn, N_Z)
-        for step in (1, 3, 2):
-            back_y[turn, step].wait_recv()
+        came(packed.at[0 : N_Y - 1, far], gy_r.at[turn])
         parts = [packed[part, far] for part in range(N_Y)]
         for place in range(N_Y):
             whole[far, place] = turn_parts(parts, [part - place for part in range(N_Y)])
-    sent = requests + picks + tiles + edges + backs
-    for copies in (over_z, back_z, back_y):
-        sent += list(copies.values())
-    for copy in sent:
-        copy.wait_send()
+    left(req_in.at[0 : N_DET - 1], req_s)
+    left(rows_out.at[0 : N_DET - 1], rows_s)
+    left(pick_in.at[0 : N_Y - 1], pick_s)
+    left(edge_out, edge_s)
+    left(sums_out.at[0 : N_Y * N_DET - 1], sums_s)
+    left(image.at[0 : N_Z - 1], rz_s)
+    left(packed.at[0, 0 : N_Z - 1], gz_s)
+    left(packed.at[0 : N_Y - 1], gy_s)
 
 
 def on_device(sky_map, tile_slot, pixel_offset, tile_list, noise_kernel):
@@ -345,8 +346,8 @@
             vmem((N_DET, SLOTS, PIX), F32),
             vmem((2, ROWS, PIX), F32),
             vmem((2, ROWS, PIX), F32),
-            vmem((N_Y, N_DET, 8, PIX), F32),
-            vmem((N_Y, N_DET, 8, PIX), F32),
+            vmem((N_Y * N_DET, 8, PIX), F32),
+            vmem((N_Y * N_DET, 8, PIX), F32),
             vmem((TILES, 2 * PIX), BF16),
             vmem((SLOT_ALL, TILES), BF16),
             vmem((TILES, N_Y * SLOT_ALL), BF16),
@@ -360,21 +361,21 @@
             vmem((ROWS, 16, PIX), F32),
             vmem((SLOT_ALL, 2 * PIX), F32),
             dma((5,)),
-            dma((N_DET,)),
-            dma((N_DET,)),
-            dma((N_Y,)),
-            dma((N_Y,)),
-            dma((N_DET,)),
-            dma((N_DET,)),
-            dma((2,)),
-            dma((2,)),
-            dma((N_Y, N_DET)),
-            dma((N_Y, N_DET)),
+            dma,
+            dma,
+            dma,
+            dma,
+            dma,
+            dma,
+            dma,
+            dma,
+            dma,
+            dma,
+            dma,
+            dma,
+            dma,
             dma((N_Z,)),
-            dma((N_Z,)),
-            dma((N_Z, N_Y)),
-            dma((N_Z, N_Y)),
-            dma((N_Z,)),
+            dma,
             dma((N_Z,)),
         ],
         compiler_params=pltpu.CompilerParams(

time: 64.5 us -> 60.1 us (0.932)
  the two profiles are of different devices: /device:TPU:8 before, /device:TPU:32 now
where the time goes in v4:
time: 60.1 us; the launch traced here: 58.9 us
  Pallas kernels  58.1 us (97%)
  local copies, waits for them, and re-layouts  0.8 us (1%)
    pallas_call x1, Pallas kernels, on_device(): pl.pallas_call(kernel, out_shape=vmem((N_Y, N_Z, SUB, PIX), F32), in_spec...  58.1 us

profile of v4, /device:TPU:32, one launch (start us, length us, event | category | flops | bytes accessed | tf_op | source)
XLA Modules:
  0.0 58.9 jit_solution(15385983163254301068)
XLA Ops:
  0.0 58.1 %shard_map.55 = f32[4,4,64,128]{3,2,1,0:T(8,128)S(1)} custom-call(f32[1024,128]{1,0:T(8,128)} %sky_h.1, s32[16,1536]{1,0:T(8,128)} %slot_h.1, s32[16,1536]{1,0:T(8,128)} %off_h.1, s32[1,1,16,32]{3,2,1,0:T(8,128)} %list_h.1, f32[16,65]{1,0:T(8,128)} %noise_h.1), custom_call_target="tpu_custom_call" | custom-call | tf_op jit(solution)/shard_map/pallas_call | solution.py:332
  58.1 0.8 %copy.7 = f32[1024,128]{1,0:T(8,128)} copy(f32[1024,128]{1,0:T(8,128)S(1)} %bitcast.1) | data formatting | bytes 1048576

commit v5 on v4

--- a/solution.py
+++ b/solution.py
@@ -21,9 +21,13 @@
 PART = PIX // N_Y
 FAR_FIRST = (8, 9, 7, 10, 6, 11, 5, 12, 4, 13, 3, 14, 2, 15, 1)
 WIDE = ROWS * PIX
+THIRDS = 3 * PIX
+HALF = SLOT_ALL // 2
 
 F32 = jnp.float32
 BF16 = jnp.bfloat16
+F8 = jnp.float8_e4m3fn
+I16 = jnp.int16
 I32 = jnp.int32
 NT = (((1,), (1,)), ((), ()))
 MESH = pl.DeviceIdType.MESH
@@ -39,8 +43,36 @@
     return lax.broadcasted_iota(I32, shape, dim)
 
 
+def thirds(values):
+    parts = []
+    for number in range(3):
+        part = values.astype(F8).astype(F32)
+        parts.append(part)
+        values = (values - part) * 16.0
+    return parts
+
+
+def from_thirds(first, second, third):
+    return first + (second + third * 0.0625) * 0.0625
+
+
+def scale_of(values):
+    most = jnp.max(jnp.max(jnp.abs(values), axis=0, keepdims=True), axis=1, keepdims=True)
+    most = jnp.maximum(most, 1e-30)
+    return 240.0 / most, most * (1.0 / 240.0)
+
+
 def one_hot(mask):
     return jnp.where(mask, 1.0, 0.0).astype(BF16)
+
+
+def repeat_row(row, count, dtype):
+    return jnp.concatenate([jnp.broadcast_to(row, (16, PIX)).astype(dtype)] * (count // 16), axis=0)
+
+
+def one_hot_rows(row, count, dtype):
+    mask = iota((count, PIX), 0).astype(I16) == repeat_row(row, count, I16)
+    return jnp.where(mask, jnp.ones((count, PIX), BF16), jnp.zeros((count, PIX), BF16)).astype(dtype)
 
 
 def build_toeplitz(noise, toeplitz):
@@ -60,27 +92,25 @@
 
 
 def build_one_hot(slot, selector, first, last):
-    rank = iota((SLOT_ALL, PIX), 0)
-
     def step(block, carry):
         span = pl.ds(pl.multiple_of(block * PIX, PIX), PIX)
         for row in range(ROWS):
-            selector[block, :, row * PIX : (row + 1) * PIX] = one_hot(rank == slot[row : row + 1, span])
+            selector[block, :, row * PIX : (row + 1) * PIX] = one_hot_rows(slot[row : row + 1, span], SLOT_ALL, F8)
         return carry
 
     lax.fori_loop(first, last, step, 0)
 
 
-def read_block(block, table, selector, off, store):
+def read_block(block, table, scale, selector, off, store):
     rank = iota((PIX, PIX), 0)
     span = pl.ds(pl.multiple_of(block * PIX, PIX), PIX)
     for row in range(0, ROWS, 4):
         both = jnp.dot(table[...], selector[block, :, row * PIX : (row + 4) * PIX], preferred_element_type=F32)
-        both = both[:PIX] + both[PIX:]
+        both = from_thirds(both[:PIX], both[PIX : 2 * PIX], both[2 * PIX :])
         for more in range(4):
             mask = rank == off[row + more : row + more + 1, span]
             part = both[:, more * PIX : (more + 1) * PIX]
-            store(row + more, jnp.sum(jnp.where(mask, part, 0.0), axis=0, keepdims=True))
+            store(row + more, jnp.sum(jnp.where(mask, part, 0.0), axis=0, keepdims=True) * scale)
 
 
 def filter_samples(samples, toeplitz, filtered):
@@ -107,21 +137,25 @@
     return result
 
 
-def scatter_samples(filtered, off, selector, total):
-    rank = iota((PIX, PIX), 0)
+def spread_block(block, parts, off):
+    span = pl.ds(pl.multiple_of(block * PIX, PIX), PIX)
+    rank = iota((PIX, PIX), 0).astype(I16)
+    zeros = jnp.zeros((PIX, PIX), BF16)
+    rows = [[], []]
+    for row in range(ROWS):
+        mask = rank == repeat_row(off[row : row + 1, span], PIX, I16)
+        for number in range(2):
+            value = repeat_row(parts[number, row, pl.ds(block, 1), :], PIX, BF16)
+            rows[number].append(jnp.where(mask, value, zeros))
+    return jnp.concatenate([jnp.concatenate(row, axis=1) for row in rows], axis=0)
+
+
+def scatter_half(start, selector, parts, off, total):
     total[...] = jnp.zeros_like(total)
 
     def step(block, carry):
-        span = pl.ds(pl.multiple_of(block * PIX, PIX), PIX)
-        highs, lows = [], []
-        for row in range(ROWS):
-            mask = rank == off[row : row + 1, span]
-            value = filtered[row, pl.ds(block, 1), :]
-            high = value.astype(BF16).astype(F32)
-            highs.append(jnp.where(mask, high, 0.0).astype(BF16))
-            lows.append(jnp.where(mask, value - high, 0.0).astype(BF16))
-        spread = jnp.concatenate([jnp.concatenate(highs, axis=1), jnp.concatenate(lows, axis=1)], axis=0)
-        total[...] += lax.dot_general(selector[block], spread, NT, preferred_element_type=F32)
+        chosen = selector[block, pl.ds(start, HALF), :].astype(BF16)
+        total[...] += lax.dot_general(spread_block(block, parts, off), chosen, NT, preferred_element_type=F32)
         return carry
 
     lax.fori_loop(0, BLOCKS, step, 0, unroll=4)
@@ -132,7 +166,7 @@
     sky, slot, off, noise,
     req_in, list_in, pick_in, rows_out, rows_in, edge_out, edge_in, sums_out, sums_in,
     sky_parts, pick_rows, pick_cols, image, part_z, packed,
-    toeplitz, selector, table, samples, filtered, total,
+    toeplitz, selector, table, samples, filtered, parts, total,
     load_sem, req_s, req_r, pick_s, pick_r, rows_s, rows_r, edge_s, edge_r, sums_s, sums_r,
     rz_s, rz_r, gz_s, gz_r, gy_s, gy_r,
 ):
@@ -228,9 +262,10 @@
     loads[4].wait()
     came(rows_in.at[0 : N_DET - 1], rows_r)
 
-    high, low = halves(rows_in[...].reshape(SLOT_ALL, PIX).T)
-    table[0:PIX, :] = high
-    table[PIX : 2 * PIX, :] = low
+    values = rows_in[...].reshape(SLOT_ALL, PIX)
+    scale, back = scale_of(values)
+    for number, part in enumerate(thirds((values * scale).T)):
+        table[number * PIX : (number + 1) * PIX, :] = part.astype(F8)
 
     for side, block in ((0, 0), (1, BLOCKS - 1)):
 
@@ -238,7 +273,7 @@
             samples[row, block + 1 : block + 2, :] = value
             edge_out[side, row : row + 1, :] = value
 
-        read_block(block, table, selector, off, keep_edge)
+        read_block(block, table, back, selector, off, keep_edge)
     remote(edge_out.at[1], edge_in.at[0], edge_s, edge_r, (group, after))
     remote(edge_out.at[0], edge_in.at[1], edge_s, edge_r, (group, before))
 
@@ -246,7 +281,7 @@
         def keep(row, value):
             samples[row, pl.ds(block + 1, 1), :] = value
 
-        read_block(block, table, selector, off, keep)
+        read_block(block, table, back, selector, off, keep)
         return carry
 
     lax.fori_loop(1, BLOCKS - 1, read_step, 0, unroll=5)
@@ -259,29 +294,42 @@
         samples[row, BLOCKS + 2 : BLOCKS + 4, :] = jnp.zeros((2, PIX), F32)
 
     filter_samples(samples, toeplitz, filtered)
-    scatter_samples(filtered, off, selector, total)
-    sums = (total[:, :PIX] + total[:, PIX:]).reshape(N_DET, N_Y, 8, PIX)
-    places = [sums[:, place].reshape(N_DET * 8, PIX) for place in range(N_Y)]
-    for part in range(N_Y):
-        turned = turn_parts(places, [place - part for place in range(N_Y)])
-        sums_out[part * N_DET : (part + 1) * N_DET] = turned.reshape(N_DET, 8, PIX)
-
-    came(pick_in.at[0 : N_Y - 1], pick_r)
-    for step in FAR_FIRST + (0,):
-        owner = lax.rem(group + step, N_DET)
-        for more in (2, 1, 3, 0):
-            if step or more:
-                part = lax.rem(y + more, N_Y)
-                remote(sums_out.at[part * N_DET + owner], sums_in.at[y * N_DET + group], sums_s, sums_r, (owner, z * N_Y + part))
+    values = filtered[...]
+    high = values.astype(BF16).astype(F32)
+    parts[0] = high
+    parts[1] = values - high
+
+    near = lax.div(group, N_DET // 2)
+    for half in (1 - near, near):
+        own = half is near
+        start = pl.multiple_of(half * HALF, HALF)
+        scatter_half(start, selector, parts, off, total)
+        sums = (total[:PIX] + total[PIX:]).T.reshape(N_DET // 2, N_Y, 8, PIX)
+        places = [sums[:, place].reshape(N_DET * 4, PIX) for place in range(N_Y)]
+        for part in range(N_Y):
+            turned = turn_parts(places, [place - part for place in range(N_Y)])
+            sums_out[pl.ds(part * N_DET + half * (N_DET // 2), N_DET // 2)] = turned.reshape(N_DET // 2, 8, PIX)
+        if not own:
+            came(pick_in.at[0 : N_Y - 1], pick_r)
+        for step in (4, 3, 5, 2, 6, 1, 7, 0):
+            owner = half * (N_DET // 2) + lax.rem(group + step, N_DET // 2)
+            for more in (2, 1, 3, 0):
+                if not own or step or more:
+                    part = lax.rem(y + more, N_Y)
+                    remote(
+                        sums_out.at[part * N_DET + owner], sums_in.at[y * N_DET + group],
+                        sums_s, sums_r, (owner, z * N_Y + part),
+                    )
     sums_in[y * N_DET + group] = sums_out[y * N_DET + group]
-    for place in range(N_Y):
-        for peer in range(N_Y):
-            start = (place * N_Y + peer) * PIX
-            pick_cols[:, start : start + PIX] = one_hot(iota((TILES, PIX), 0) == pick_in[peer, place : place + 1, :])
+    for peer in range(N_Y):
+        for place in range(N_Y):
+            chosen = one_hot_rows(pick_in[peer, place : place + 1, :], TILES, BF16)
+            start = (peer * N_Y + place) * PIX
+            pick_cols[:, start : start + PIX] = chosen
     came(sums_in.at[0 : N_Y * N_DET - 1], sums_r)
-    rows = sums_in[...].reshape(N_Y * N_DET * 8, PIX)
-    rows = jnp.concatenate([jnp.where(lane_part() == place, rows, 0.0) for place in range(N_Y)], axis=0)
-    high, low = halves(rows)
+    rows = sums_in[...].reshape(N_Y, N_DET * 8, PIX)
+    rows = [jnp.where(lane_part() == place, rows[peer], 0.0) for peer in range(N_Y) for place in range(N_Y)]
+    high, low = halves(jnp.concatenate(rows, axis=0))
     both = jnp.dot(pick_cols[...], jnp.concatenate([high, low], axis=1), preferred_element_type=F32)
     both = both[:, :PIX] + both[:, PIX:]
     both = both + pltpu.roll(both, 2 * PART, 1)
@@ -355,11 +403,12 @@
             vmem((N_Z, SUB, PIX), F32),
             vmem((N_Y, N_Z, SUB, PIX), F32),
             vmem((ROWS, 2 * PIX, 2 * PIX), BF16),
-            vmem((BLOCKS, SLOT_ALL, WIDE), BF16),
-            vmem((2 * PIX, SLOT_ALL), BF16),
+            vmem((BLOCKS, SLOT_ALL, WIDE), F8),
+            vmem((THIRDS, SLOT_ALL), F8),
             vmem((ROWS, 16, PIX), F32),
             vmem((ROWS, 16, PIX), F32),
-            vmem((SLOT_ALL, 2 * PIX), F32),
+            vmem((2, ROWS, 16, PIX), F32),
+            vmem((2 * PIX, HALF), F32),
             dma((5,)),
             dma,
             dma,

time: 60.1 us -> 58.8 us (0.978); the launches traced: 58.9 us -> 58.8 us
  no operation moved by 1% of the time
where the time goes in v5:
time: 58.8 us
  Pallas kernels  58 us (99%)
  local copies, waits for them, and re-layouts  0.8 us (1%)
    pallas_call x1, Pallas kernels, on_device(): pl.pallas_call(kernel, out_shape=vmem((N_Y, N_Z, SUB, PIX), F32), in_spec...  58 us

profile of v5, /device:TPU:32, one launch (start us, length us, event | category | flops | bytes accessed | tf_op | source)
XLA Modules:
  0.0 58.8 jit_solution(14832970833962512283)
XLA Ops:
  0.0 58.0 %shard_map.55 = f32[4,4,64,128]{3,2,1,0:T(8,128)S(1)} custom-call(f32[1024,128]{1,0:T(8,128)} %sky_h.1, s32[16,1536]{1,0:T(8,128)} %slot_h.1, s32[16,1536]{1,0:T(8,128)} %off_h.1, s32[1,1,16,32]{3,2,1,0:T(8,128)} %list_h.1, f32[16,65]{1,0:T(8,128)} %noise_h.1), custom_call_target="tpu_custom_call" | custom-call | tf_op jit(solution)/shard_map/pallas_call | solution.py:380
  58.0 0.8 %copy.7 = f32[1024,128]{1,0:T(8,128)} copy(f32[1024,128]{1,0:T(8,128)S(1)} %bitcast.1) | data formatting | bytes 1048576

commit v6 on v5

--- a/solution.py
+++ b/solution.py
@@ -104,10 +104,10 @@
 def read_block(block, table, scale, selector, off, store):
     rank = iota((PIX, PIX), 0)
     span = pl.ds(pl.multiple_of(block * PIX, PIX), PIX)
-    for row in range(0, ROWS, 4):
-        both = jnp.dot(table[...], selector[block, :, row * PIX : (row + 4) * PIX], preferred_element_type=F32)
+    for row in range(0, ROWS, 8):
+        both = jnp.dot(table[...], selector[block, :, row * PIX : (row + 8) * PIX], preferred_element_type=F32)
         both = from_thirds(both[:PIX], both[PIX : 2 * PIX], both[2 * PIX :])
-        for more in range(4):
+        for more in range(8):
             mask = rank == off[row + more : row + more + 1, span]
             part = both[:, more * PIX : (more + 1) * PIX]
             store(row + more, jnp.sum(jnp.where(mask, part, 0.0), axis=0, keepdims=True) * scale)
@@ -338,7 +338,7 @@
     for far in range(N_Z):
         image[far] = turn_parts([both[far, place] for place in range(N_Y)], [0] * N_Y)
 
-    for turn in (2, 1, 3):
+    for turn in (1, 3, 2):
         far = lax.rem(z + turn, N_Z)
         remote(image.at[far], part_z.at[z], rz_s, rz_r, (group, far * N_Y + y))
     came(part_z.at[0 : N_Z - 1], rz_r)
@@ -347,14 +347,14 @@
         value = value + part_z[lax.rem(z + N_Z - turn, N_Z)]
     packed[y, z] = value
 
-    for turn in (2, 1, 3):
+    for turn in (1, 3, 2):
         far = lax.rem(z + turn, N_Z)
         remote(packed.at[y, z], packed.at[y, z], gz_s, gz_r.at[turn], (group, far * N_Y + y))
     for turn in (0, 1, 3, 2):
         far = lax.rem(z + N_Z - turn, N_Z)
         if turn:
             came(packed.at[y, far], gz_r.at[turn])
-        for step in (2, 1, 3):
+        for step in (1, 3, 2):
             peer = lax.rem(y + step, N_Y)
             remote(packed.at[y, far], packed.at[y, far], gy_s, gy_r.at[turn], (group, z * N_Y + peer))
     for turn in (0, 1, 3, 2):

time: 58.8 us -> 58.3 us (level)
  Pallas kernels: 58 us -> 57.4 us
where the time goes in v6:
time: 58.3 us; the launch traced here: 58.2 us
  Pallas kernels  57.4 us (98%)
  local copies, waits for them, and re-layouts  0.8 us (1%)
    pallas_call x1, Pallas kernels, on_device(): pl.pallas_call(kernel, out_shape=vmem((N_Y, N_Z, SUB, PIX), F32), in_spec...  57.4 us

profile of v6, /device:TPU:32, one launch (start us, length us, event | category | flops | bytes accessed | tf_op | source)
XLA Modules:
  0.0 58.2 jit_solution(12822836522843114789)
XLA Ops:
  0.0 57.4 %shard_map.55 = f32[4,4,64,128]{3,2,1,0:T(8,128)S(1)} custom-call(f32[1024,128]{1,0:T(8,128)} %sky_h.1, s32[16,1536]{1,0:T(8,128)} %slot_h.1, s32[16,1536]{1,0:T(8,128)} %off_h.1, s32[1,1,16,32]{3,2,1,0:T(8,128)} %list_h.1, f32[16,65]{1,0:T(8,128)} %noise_h.1), custom_call_target="tpu_custom_call" | custom-call | tf_op jit(solution)/shard_map/pallas_call | solution.py:380
  57.5 0.8 %copy.7 = f32[1024,128]{1,0:T(8,128)} copy(f32[1024,128]{1,0:T(8,128)S(1)} %bitcast.1) | data formatting | bytes 1048576

commit v7 on v6

--- a/solution.py
+++ b/solution.py
@@ -341,6 +341,11 @@
     for turn in (1, 3, 2):
         far = lax.rem(z + turn, N_Z)
         remote(image.at[far], part_z.at[z], rz_s, rz_r, (group, far * N_Y + y))
+    left(req_in.at[0 : N_DET - 1], req_s)
+    left(rows_out.at[0 : N_DET - 1], rows_s)
+    left(pick_in.at[0 : N_Y - 1], pick_s)
+    left(edge_out, edge_s)
+    left(sums_out.at[0 : N_Y * N_DET - 1], sums_s)
     came(part_z.at[0 : N_Z - 1], rz_r)
     value = image[z]
     for turn in (1, 3, 2):
@@ -352,6 +357,8 @@
         remote(packed.at[y, z], packed.at[y, z], gz_s, gz_r.at[turn], (group, far * N_Y + y))
     for turn in (0, 1, 3, 2):
         far = lax.rem(z + N_Z - turn, N_Z)
+        if turn == 1:
+            left(image.at[0 : N_Z - 1], rz_s)
         if turn:
             came(packed.at[y, far], gz_r.at[turn])
         for step in (1, 3, 2):
@@ -363,12 +370,6 @@
         parts = [packed[part, far] for part in range(N_Y)]
         for place in range(N_Y):
             whole[far, place] = turn_parts(parts, [part - place for part in range(N_Y)])
-    left(req_in.at[0 : N_DET - 1], req_s)
-    left(rows_out.at[0 : N_DET - 1], rows_s)
-    left(pick_in.at[0 : N_Y - 1], pick_s)
-    left(edge_out, edge_s)
-    left(sums_out.at[0 : N_Y * N_DET - 1], sums_s)
-    left(image.at[0 : N_Z - 1], rz_s)
     left(packed.at[0, 0 : N_Z - 1], gz_s)
     left(packed.at[0 : N_Y - 1], gy_s)
 

time: 58.3 us -> 58.3 us (level)
  no operation moved by 1% of the time
where the time goes in v7:
time: 58.3 us; the launch traced here: 58.2 us
  Pallas kernels  57.4 us (98%)
  local copies, waits for them, and re-layouts  0.8 us (1%)
    pallas_call x1, Pallas kernels, on_device(): pl.pallas_call(kernel, out_shape=vmem((N_Y, N_Z, SUB, PIX), F32), in_spec...  57.4 us

profile of v7, /device:TPU:32, one launch (start us, length us, event | category | flops | bytes accessed | tf_op | source)
XLA Modules:
  0.0 58.2 jit_solution(13930302374189747158)
XLA Ops:
  0.0 57.4 %shard_map.55 = f32[4,4,64,128]{3,2,1,0:T(8,128)S(1)} custom-call(f32[1024,128]{1,0:T(8,128)} %sky_h.1, s32[16,1536]{1,0:T(8,128)} %slot_h.1, s32[16,1536]{1,0:T(8,128)} %off_h.1, s32[1,1,16,32]{3,2,1,0:T(8,128)} %list_h.1, f32[16,65]{1,0:T(8,128)} %noise_h.1), custom_call_target="tpu_custom_call" | custom-call | tf_op jit(solution)/shard_map/pallas_call | solution.py:381
  57.4 0.8 %copy.7 = f32[1024,128]{1,0:T(8,128)} copy(f32[1024,128]{1,0:T(8,128)S(1)} %bitcast.1) | data formatting | bytes 1048576
